TPU v7x, 128 devices: a whole 4x4x4 slice. The times are simulated.
128 devices in a mesh: dp: 4 (over x), fsdp: 4 (over z_hi, core), seq: 8 (over z_lo, y).
Axes of the slice: x: 4, y: 4, z: 4 (z_hi: 2, z_lo: 2; z = z_hi * 2 + z_lo), core: 2. Of those that a mesh axis runs over, the one named last changes fastest.
Arguments:
- frames: bfloat16 [16, 2048, 1536], P(('dp', 'fsdp'), 'seq'), may hold values from -6 to 6
- projection: bfloat16 [1536, 3072], P('fsdp'), may hold values from -1 to 1
- lengths: int32 [16], P(('dp', 'fsdp')), may hold values from 512 to 2048
- cotangent: bfloat16 [16, 2048, 1024], P(('dp', 'fsdp'), 'seq'), may hold values from -24 to 24
Outputs:
- context: bfloat16 [16, 2048, 1024], P(('dp', 'fsdp'), 'seq')
- input_gradient: float32 [16, 2048, 1536], P(('dp', 'fsdp'), 'seq')
- projection_gradient: float32 [1536, 3072], P(('dp', 'fsdp', 'seq'))
All inputs are finite; a program needn't handle non-finite values.
Results may differ from a plain program's by a relative error of at most 0.007.
The roundings to bfloat16 on the way count: a program that leaves them out, or rounds other values in their place, can miss the bound.
Values may be sent and summed in bfloat16 or wider, within the bound.
No kernel may reach another device: no remote copies, remote signals or barrier semaphores. Data moves between devices by JAX's collectives and lax.ppermute only.
A program may use at most 128 MiB of HBM per device.

v0:
```python
import math
import jax
import jax.numpy as jnp
from jax import lax
from jax.sharding import PartitionSpec as P

HEADS = 16
HD = 64
EPS = 1e-05


def block_probabilities(query_block, key_rows, valid):
    factor = 1.0 / math.sqrt(query_block.shape[-1])
    scores = (
        jnp.einsum("qhd,khd->hqk", query_block, key_rows, preferred_element_type=jnp.float32)
        * factor
    )
    scores = jnp.where(valid[None, None, :], scores, -jnp.inf)
    row_peak = jnp.max(scores, axis=2, keepdims=True)
    exponentials = jnp.exp(scores - row_peak)
    return exponentials / jnp.sum(exponentials, axis=2, keepdims=True)


def forward_heads(query_rows, key_rows, value_rows, valid, block_rows):
    total_rows = query_rows.shape[0]

    def forward_one_block(block_index):
        first_row = block_index * block_rows
        query_block = lax.dynamic_slice_in_dim(query_rows, first_row, block_rows, 0)
        probabilities = block_probabilities(query_block, key_rows, valid)
        mixture = jnp.einsum(
            "hqk,khd->qhd",
            probabilities.astype(jnp.bfloat16),
            value_rows,
            preferred_element_type=jnp.float32,
        )
        keep_rows = lax.dynamic_slice_in_dim(valid, first_row, block_rows, 0)
        return jnp.where(keep_rows[:, None, None], mixture, jnp.zeros_like(mixture)).astype(
            jnp.bfloat16
        )

    blocks = lax.map(forward_one_block, jnp.arange(total_rows // block_rows, dtype=jnp.int32))
    return blocks.reshape(query_rows.shape)


def backward_heads(query_rows, key_rows, value_rows, upstream, valid, block_rows):
    total_rows = query_rows.shape[0]
    factor = 1.0 / math.sqrt(query_rows.shape[-1])

    def backward_one_block(running, block_index):
        key_sum, value_sum = running
        first_row = block_index * block_rows
        query_block = lax.dynamic_slice_in_dim(query_rows, first_row, block_rows, 0)
        upstream_block = lax.dynamic_slice_in_dim(upstream, first_row, block_rows, 0)
        keep_rows = lax.dynamic_slice_in_dim(valid, first_row, block_rows, 0)
        upstream_block = jnp.where(
            keep_rows[:, None, None], upstream_block, jnp.zeros_like(upstream_block)
        )
        probabilities = block_probabilities(query_block, key_rows, valid)
        value_sum = value_sum + jnp.einsum(
            "hqk,qhd->khd",
            probabilities.astype(jnp.bfloat16),
            upstream_block,
            preferred_element_type=jnp.float32,
        )
        prob_gradient = jnp.einsum(
            "qhd,khd->hqk", upstream_block, value_rows, preferred_element_type=jnp.float32
        )
        row_inner = jnp.sum(probabilities * prob_gradient, axis=2, keepdims=True)
        score_gradient = (probabilities * (prob_gradient - row_inner) * factor).astype(jnp.bfloat16)
        query_gradient = jnp.einsum(
            "hqk,khd->qhd", score_gradient, key_rows, preferred_element_type=jnp.float32
        ).astype(jnp.bfloat16)
        key_sum = key_sum + jnp.einsum(
            "hqk,qhd->khd", score_gradient, query_block, preferred_element_type=jnp.float32
        )
        return ((key_sum, value_sum), query_gradient)

    empty_sum = jnp.zeros(key_rows.shape, jnp.float32)
    sums, query_blocks = lax.scan(
        backward_one_block,
        (empty_sum, empty_sum),
        jnp.arange(total_rows // block_rows, dtype=jnp.int32),
    )
    return (
        query_blocks.reshape(query_rows.shape),
        sums[0].astype(jnp.bfloat16),
        sums[1].astype(jnp.bfloat16),
    )


def body(frames, projection, lengths, cotangent):
    inputs = frames[0]
    upstream = cotangent[0]
    length = lengths[0]
    seq_count = lax.axis_size("seq")
    local_rows, feature_count = inputs.shape
    total_rows = local_rows * seq_count
    head_count = HEADS // seq_count
    group_width = head_count * HD
    block_rows = 512
    as_float = inputs.astype(jnp.float32)
    centered = as_float - jnp.mean(as_float, axis=1, keepdims=True)
    inv_std = lax.rsqrt(jnp.mean(centered * centered, axis=1, keepdims=True) + EPS)
    standard = centered * inv_std
    normed = standard.astype(jnp.bfloat16)
    valid = jnp.arange(total_rows, dtype=jnp.int32) < length
    weight_full = lax.all_gather(projection, "fsdp", axis=0, tiled=True)
    packed = jnp.dot(normed, weight_full, preferred_element_type=jnp.float32).astype(jnp.bfloat16)
    packed = packed.reshape(local_rows, 3, seq_count, group_width)
    upstream_four = upstream.reshape(local_rows, 1, seq_count, group_width)
    head_inputs, head_upstream = (
        lax.all_to_all(packed, "seq", split_axis=2, concat_axis=0, tiled=True),
        lax.all_to_all(upstream_four, "seq", split_axis=2, concat_axis=0, tiled=True),
    )
    head_inputs = head_inputs.reshape(total_rows, 3, head_count, HD)
    head_grads = head_upstream.reshape(total_rows, head_count, HD)
    query_rows = head_inputs[:, 0]
    key_rows = head_inputs[:, 1]
    value_rows = head_inputs[:, 2]
    mixture = forward_heads(query_rows, key_rows, value_rows, valid, block_rows)
    returned_context = lax.all_to_all(
        mixture.reshape(total_rows, 1, group_width), "seq", split_axis=0, concat_axis=1, tiled=True
    )
    context = returned_context.reshape(local_rows, seq_count * group_width)
    query_gradient, key_gradient, value_gradient = backward_heads(
        query_rows, key_rows, value_rows, head_grads, valid, block_rows
    )
    stacked = jnp.stack([query_gradient, key_gradient, value_gradient], axis=1).reshape(
        total_rows, 3, 1, group_width
    )
    returned = lax.all_to_all(stacked, "seq", split_axis=0, concat_axis=2, tiled=True)
    packed_gradient = returned.reshape(local_rows, 3 * seq_count * group_width)
    normed_gradient = lax.dot_general(
        packed_gradient, weight_full, (((1,), (1,)), ((), ())), preferred_element_type=jnp.float32
    )
    projection_gradient = lax.psum_scatter(
        lax.dot_general(
            normed, packed_gradient, (((0,), (0,)), ((), ())), preferred_element_type=jnp.float32
        ),
        ("dp", "fsdp", "seq"),
        scatter_dimension=0,
        tiled=True,
    )
    row_mean = jnp.mean(normed_gradient, axis=1, keepdims=True)
    projected = jnp.mean(normed_gradient * standard, axis=1, keepdims=True)
    input_gradient = inv_std * (normed_gradient - row_mean - standard * projected)
    return (context[None], input_gradient[None], projection_gradient)


def solution(mesh):
    placed = (
        P(("dp", "fsdp"), "seq", None),
        P("fsdp", None),
        P(("dp", "fsdp")),
        P(("dp", "fsdp"), "seq", None),
    )
    return jax.shard_map(
        body,
        mesh=mesh,
        in_specs=placed,
        out_specs=(
            P(("dp", "fsdp"), "seq", None),
            P(("dp", "fsdp"), "seq", None),
            P(("dp", "fsdp", "seq"), None),
        ),
        check_vma=False,
    )
```

profile of v0, /device:TPU:2, one launch (start us, length us, event | category | flops | bytes accessed | tf_op | source)
XLA Modules:
  0.0 1038.3 jit_solution(2263338651254375848)
XLA Ops:
  9.9 5.8 all-to-all-start.2
  18.6 61.9 %all-gather.2.cloned.1.call-done = bf16[1536,3072]{1,0:T(8,128)(2,1)} async-done(((bf16[384,3072]{1,0:T(8,128)(2,1)}), bf16[1536,3072]{1,0:T(8,128)(2,1)}) %all-gather.2.cloned.1.call-update) | async-done | bytes 9437200 | tf_op jit(solution)/shard_map/all_gather | solution.py:108
  80.5 6.7 fusion.105
  89.0 4.4 all-to-all-start
  94.6 20.5 %all-to-all-done = bf16[256,3,8,128]{3,0,1,2:T(8,128)(2,1)S(1)} async-done(((bf16[256,3,8,128]{3,0,1,2:T(8,128)(2,1)}), bf16[256,3,8,128]{3,0,1,2:T(8,128)(2,1)S(1)}, u32[]{:S(2)}, u32[]{:S(2)}) %all-to-all-start) | async-done | bytes 1572896 | tf_op jit(solution)/shard_map/all_to_all | solution.py:113
  116.9 2.6 reshape.79
  120.5 197.0 %while.26 = (s32[]{:T(128)}, f32[2048,2,64]{0,2,1:T(8,128)}, f32[2048,2,64]{0,2,1:T(8,128)}, bf16[4,512,2,64]{1,3,2,0:T(8,128)(2,1)S(1)}, s32[4]{0:T(128)S(1)}, ...) while((s32[]{:T(128)}, f32[2048,2,64]{0,2,1:T(8,128)}, ...), condition=%wide.region_10.11_spmd.clone, body=%wide.region_6.10_spmd.clone.sunk | while | flops 1385373696 | bytes 107115288 | solution.py:80
  121.8 4.6 fusion.167
  126.4 6.6 fusion.168
  132.9 14.4 %fusion.171 = bf16[4,512,2,64]{1,3,2,0:T(8,128)(2,1)S(1)} fusion(bf16[4,512,2,64]{1,3,2,0:T(8,128)(2,1)S(1)} %get-tuple-element.351, s32[]{:T(128)} %get-tuple-element.348, bf16[2048,2,64]{0,2,1:T(8,128)(2,1)S(1)} %get-tuple-element.369, f32[2,512,2048]{2,1,0:T(8,128)} %fusion.167, f32[2,512,2048]{2,1,0:T(8,128)} %get-tuple-element.299, ...), kind=kOutput, calls=%fused_computation.43.clone.1 | convolution fusion | flops 283184128 | bytes 34218496 | tf_op jit(solution)/shard_map/while/body/eval_jaxpr/hqk,khd->qhd/dot_general | solution.py:71
  147.4 5.4 fusion.170
  152.8 15.8 %fusion.169 = f32[2048,2,64]{0,2,1:T(8,128)S(1)} fusion(f32[2,512,2048]{2,1,0:T(8,128)} %fusion.167, f32[2048,2,64]{0,2,1:T(8,128)S(1)} %copy-done.1, pred[]{:T(512)S(6)} %compare.3, bf16[2048,2,64]{0,2,1:T(8,128)(2,1)} %get-tuple-element.367, s32[]{:T(128)S(6)} %select_n.71, f32[2,512,2048]{2,1,0:T(8,128)} %get-tuple-element.299, ...), kind=kOutput, calls=%fused_computation.40.clone.1 | convolution fusion | flops 283642880 | bytes 35790852 | tf_op jit(solution)/shard_map/while/body/eval_jaxpr/hqk,qhd->khd/dot_general | solution.py:74
  170.9 4.6 fusion.167
  175.4 6.6 fusion.168
  182.0 14.4 %fusion.171 = bf16[4,512,2,64]{1,3,2,0:T(8,128)(2,1)S(1)} fusion(bf16[4,512,2,64]{1,3,2,0:T(8,128)(2,1)S(1)} %get-tuple-element.351, s32[]{:T(128)} %get-tuple-element.348, bf16[2048,2,64]{0,2,1:T(8,128)(2,1)S(1)} %get-tuple-element.369, f32[2,512,2048]{2,1,0:T(8,128)} %fusion.167, f32[2,512,2048]{2,1,0:T(8,128)} %get-tuple-element.299, ...), kind=kOutput, calls=%fused_computation.43.clone.1 | convolution fusion | flops 283184128 | bytes 34218496 | tf_op jit(solution)/shard_map/while/body/eval_jaxpr/hqk,khd->qhd/dot_general | solution.py:71
  196.4 5.6 fusion.170
  202.1 15.8 %fusion.169 = f32[2048,2,64]{0,2,1:T(8,128)S(1)} fusion(f32[2,512,2048]{2,1,0:T(8,128)} %fusion.167, f32[2048,2,64]{0,2,1:T(8,128)S(1)} %copy-done.1, pred[]{:T(512)S(6)} %compare.3, bf16[2048,2,64]{0,2,1:T(8,128)(2,1)} %get-tuple-element.367, s32[]{:T(128)S(6)} %select_n.71, f32[2,512,2048]{2,1,0:T(8,128)} %get-tuple-element.299, ...), kind=kOutput, calls=%fused_computation.40.clone.1 | convolution fusion | flops 283642880 | bytes 35790852 | tf_op jit(solution)/shard_map/while/body/eval_jaxpr/hqk,qhd->khd/dot_general | solution.py:74
  220.2 4.6 fusion.167
  224.8 6.6 fusion.168
  231.3 14.4 %fusion.171 = bf16[4,512,2,64]{1,3,2,0:T(8,128)(2,1)S(1)} fusion(bf16[4,512,2,64]{1,3,2,0:T(8,128)(2,1)S(1)} %get-tuple-element.351, s32[]{:T(128)} %get-tuple-element.348, bf16[2048,2,64]{0,2,1:T(8,128)(2,1)S(1)} %get-tuple-element.369, f32[2,512,2048]{2,1,0:T(8,128)} %fusion.167, f32[2,512,2048]{2,1,0:T(8,128)} %get-tuple-element.299, ...), kind=kOutput, calls=%fused_computation.43.clone.1 | convolution fusion | flops 283184128 | bytes 34218496 | tf_op jit(solution)/shard_map/while/body/eval_jaxpr/hqk,khd->qhd/dot_general | solution.py:71
  245.7 5.6 fusion.170
  251.4 15.8 %fusion.169 = f32[2048,2,64]{0,2,1:T(8,128)S(1)} fusion(f32[2,512,2048]{2,1,0:T(8,128)} %fusion.167, f32[2048,2,64]{0,2,1:T(8,128)S(1)} %copy-done.1, pred[]{:T(512)S(6)} %compare.3, bf16[2048,2,64]{0,2,1:T(8,128)(2,1)} %get-tuple-element.367, s32[]{:T(128)S(6)} %select_n.71, f32[2,512,2048]{2,1,0:T(8,128)} %get-tuple-element.299, ...), kind=kOutput, calls=%fused_computation.40.clone.1 | convolution fusion | flops 283642880 | bytes 35790852 | tf_op jit(solution)/shard_map/while/body/eval_jaxpr/hqk,qhd->khd/dot_general | solution.py:74
  269.5 4.6 fusion.167
  274.1 6.6 fusion.168
  280.7 14.4 %fusion.171 = bf16[4,512,2,64]{1,3,2,0:T(8,128)(2,1)S(1)} fusion(bf16[4,512,2,64]{1,3,2,0:T(8,128)(2,1)S(1)} %get-tuple-element.351, s32[]{:T(128)} %get-tuple-element.348, bf16[2048,2,64]{0,2,1:T(8,128)(2,1)S(1)} %get-tuple-element.369, f32[2,512,2048]{2,1,0:T(8,128)} %fusion.167, f32[2,512,2048]{2,1,0:T(8,128)} %get-tuple-element.299, ...), kind=kOutput, calls=%fused_computation.43.clone.1 | convolution fusion | flops 283184128 | bytes 34218496 | tf_op jit(solution)/shard_map/while/body/eval_jaxpr/hqk,khd->qhd/dot_general | solution.py:71
  295.1 5.6 fusion.170
  300.7 15.8 %fusion.169 = f32[2048,2,64]{0,2,1:T(8,128)S(1)} fusion(f32[2,512,2048]{2,1,0:T(8,128)} %fusion.167, f32[2048,2,64]{0,2,1:T(8,128)S(1)} %copy-done.1, pred[]{:T(512)S(6)} %compare.3, bf16[2048,2,64]{0,2,1:T(8,128)(2,1)} %get-tuple-element.367, s32[]{:T(128)S(6)} %select_n.71, f32[2,512,2048]{2,1,0:T(8,128)} %get-tuple-element.299, ...), kind=kOutput, calls=%fused_computation.40.clone.1 | convolution fusion | flops 283642880 | bytes 35790852 | tf_op jit(solution)/shard_map/while/body/eval_jaxpr/hqk,qhd->khd/dot_general | solution.py:74
  322.2 3.0 copy.54
  325.3 30.3 %all_to_all.60 = bf16[2048,3,1,128]{3,1,2,0:T(4,128)(2,1)S(1)} all-to-all(bf16[2048,3,1,128]{3,1,2,0:T(4,128)(2,1)S(1)} %copy.54), channel_id=1, replica_groups=mesh['dp'=4,'fsdp'=4,'seq'=8] {'seq'}, dimensions={0} | all-to-all | bytes 3145728 | tf_op jit(solution)/shard_map/all_to_all | solution.py:132
  358.7 8.0 fusion.107
  366.7 325.4 %fusion = f32[16,3072]{1,0:T(8,128)} fusion(f32[1536,3072]{1,0:T(8,128)} %fusion.107), kind=kCustom, calls=%all-reduce-scatter | all-reduce-scatter fusion | flops 6291457 | bytes 19070976
  692.2 3.4 collective-permute-start
  696.6 4.1 collective-permute-start.31
  704.5 6.7 collective-permute-start.11
  711.2 33.2 %collective-permute-done.31 = f32[12,3072]{1,0:T(8,128)S(1)} collective-permute-done((f32[12,3072]{1,0:T(8,128)S(1)}, f32[12,3072]{1,0:T(8,128)S(1)}, u32[]{:S(2)}, u32[]{:S(2)}) %collective-permute-start.31) | collective-permute-done | bytes 147488
  748.4 51.9 %while.25 = (s32[]{:T(128)}, bf16[4,512,2,64]{1,3,2,0:T(8,128)(2,1)S(1)}, s32[4]{0:T(128)S(1)}, pred[2048]{0:T(1024)(128)(4,1)S(1)}, bf16[2048,2,64]{0,2,1:T(8,1...) while((s32[]{:T(128)}, ...), condition=%wide.region_5.6_spmd, body=%wide.region_2.5_spmd.sunk | while | flops 549586944 | bytes 18099892 | solution.py:42
  749.6 6.9 fusion.157
  756.5 4.8 fusion.158
  762.5 6.9 fusion.157
  769.5 4.8 fusion.158
  775.5 6.9 fusion.157
  782.4 4.8 fusion.158
  788.5 6.9 fusion.157
  795.4 4.8 fusion.158
  802.2 5.0 reshape.82
  807.7 12.6 %reduce.1 = bf16[2048,128]{1,0:T(8,128)(2,1)S(1)} reduce(bf16[2048,1,128]{2,1,0:T(2,128)(2,1)} %reshape.82, bf16[]{:T(256)} %broadcast.123), dimensions={1}, to_apply=%reshape.82.reduce_sub_computation | reduce | bytes 1048578 | tf_op jit(solution)/shard_map/reshape;reshape | solution.py:123
  821.2 3.5 all-to-all-start.1
  824.7 13.4 %collective-permute-start.14 = (f32[16,3072]{1,0:T(8,128)}, f32[16,3072]{1,0:T(8,128)}, u32[]{:S(2)}, u32[]{:S(2)}) collective-permute-start(f32[16,3072]{1,0:T(8,128)} %fusion), channel_id=1, source_target_pairs={{0,15},{1,16},{2,17},{3,18},{4,19},{5,20},{6,21},{7,22},{8,23},{9,... | collective-permute-start | bytes 589832
  840.1 3.9 collective-permute-start.16
  844.0 4.9 collective-permute-start.17
  848.9 2.2 collective-permute-start.18
  853.1 9.9 collective-permute-start.2
  863.1 5.8 collective-permute-start.20
  868.9 5.6 collective-permute-start.21
  884.8 5.5 collective-permute-start.25
  894.4 5.5 fusion.114
  903.8 2.8 collective-permute-start.3
  911.0 2.3 collective-permute-done.28
  913.3 6.2 collective-permute-start.5
  919.5 4.9 collective-permute-start.6
  924.4 3.9 collective-permute-start.7
  930.3 5.6 collective-permute-start.9
  937.5 6.3 collective-permute-done.8
  945.8 84.0 %concatenate.1 = f32[524,3072]{1,0:T(8,128)} concatenate(f32[12,3072]{1,0:T(8,128)S(1)} %copy-done.7, f32[16,3072]{1,0:T(8,128)S(1)} %collective-permute-done.30, f32[16,3072]{1,0:T(8,128)S(1)} %collective-permute-done.29, f32[16,3072]{1,0:T(8,128)S(1)} %collective-permute-done.28, f32[16,3072]{1,0:T(8,128)} %copy-done.9, f32[16,3072]{1,0:T(8,128)} %copy-done.8, ...), dimensions={0} | concatenate | bytes 12877824
  (141 shorter events, 73.5 us)
Async XLA Ops:
  7.2 73.3 %all-gather.2.cloned.1.call-start = ((), (), s32[]{:S(2)}) async-start(), calls=%async_computation.4 | async-start | bytes 11796480 | tf_op jit(solution)/shard_map/all_gather | solution.py:108
  9.9 79.0 %all-to-all-start.2 = ((bf16[256,1,8,128]{0,3,1,2:T(8,128)(2,1)}), bf16[256,1,8,128]{0,3,1,2:T(8,128)(2,1)S(1)}, u32[]{:S(2)}, u32[]{:S(2)}) async-start(bf16[256,1,8,128]{0,3,1,2:T(8,128)(2,1)} %bitcast.12), calls=%async_computation.2 | async-start | bytes 1048576 | tf_op jit(solution)/shard_map/all_to_all | solution.py:114
  17.1 70.1 %copy-start.10 = (f32[256]{0:T(256)}, f32[256]{0:T(256)S(1)}, u32[]{:S(2)}) copy-start(f32[256]{0:T(256)S(1)} %broadcast_multiply_fusion.2) | copy-start | bytes 3076
  18.6 68.6 %copy-start.12 = (f32[256]{0:T(256)}, f32[256]{0:T(256)S(1)}, u32[]{:S(2)}) copy-start(f32[256]{0:T(256)S(1)} %add_rsqrt_fusion) | copy-start | bytes 3076
  89.0 26.1 %all-to-all-start = ((bf16[256,3,8,128]{3,0,1,2:T(8,128)(2,1)}), bf16[256,3,8,128]{3,0,1,2:T(8,128)(2,1)S(1)}, u32[]{:S(2)}, u32[]{:S(2)}) async-start(bf16[256,3,8,128]{3,0,1,2:T(8,128)(2,1)} %copy.46), calls=%async_computation | async-start | bytes 3145728 | tf_op jit(solution)/shard_map/all_to_all | solution.py:113
  147.3 5.4 copy-start.1
  168.5 1.0 copy-start.2
  196.4 5.7 copy-start.1
  217.9 1.0 copy-start.2
  245.7 5.6 copy-start.1
  267.2 1.0 copy-start.2
  295.1 5.7 copy-start.1
  316.5 1.0 copy-start.2
  317.5 3.4 copy-start.3
  320.9 37.8 %copy-start = (bf16[1,256,1536]{2,1,0:T(8,128)(2,1)S(1)}, bf16[1,256,1536]{2,1,0:T(8,128)(2,1)}, u32[]{:S(2)}) copy-start(bf16[1,256,1536]{2,1,0:T(8,128)(2,1)} %param.8) | copy-start | bytes 2359300
  320.9 37.8 %copy-start.11 = (f32[256]{0:T(256)S(1)}, f32[256]{0:T(256)}, u32[]{:S(2)}) copy-start(f32[256]{0:T(256)} %copy-done.10) | copy-start | bytes 3076
  320.9 37.8 %copy-start.13 = (f32[256]{0:T(256)S(1)}, f32[256]{0:T(256)}, u32[]{:S(2)}) copy-start(f32[256]{0:T(256)} %copy-done.12) | copy-start | bytes 3076
  692.2 54.2 %collective-permute-start = (f32[16,3072]{1,0:T(8,128)}, f32[16,3072]{1,0:T(8,128)S(1)}, u32[]{:S(2)}, u32[]{:S(2)}) collective-permute-start(f32[16,3072]{1,0:T(8,128)} %fusion), channel_id=1, source_target_pairs={{0,1},{1,2},{2,3},{3,4},{4,5},{5,6},{6,7},{7,8},{8,9},{9,10},{10,1... | collective-permute-start | bytes 589832
  696.6 47.9 %collective-permute-start.31 = (f32[12,3072]{1,0:T(8,128)S(1)}, f32[12,3072]{1,0:T(8,128)S(1)}, u32[]{:S(2)}, u32[]{:S(2)}) collective-permute-start(f32[12,3072]{1,0:T(8,128)S(1)} %slice.15), channel_id=1, source_target_pairs={{0,32},{1,33},{2,34},{3,35},{4,36},{5,37},{6,38},{7,39},{8,40},{9,... | collective-permute-start | bytes 442376
  700.6 124.1 %collective-permute-start.1 = (f32[16,3072]{1,0:T(8,128)}, f32[16,3072]{1,0:T(8,128)}, u32[]{:S(2)}, u32[]{:S(2)}) collective-permute-start(f32[16,3072]{1,0:T(8,128)} %fusion), channel_id=1, source_target_pairs={{0,2},{1,3},{2,4},{3,5},{4,6},{5,7},{6,8},{7,9},{8,10},{9,11},{10,... | collective-permute-start | bytes 589832
  702.6 135.5 %collective-permute-start.10 = (f32[16,3072]{1,0:T(8,128)}, f32[16,3072]{1,0:T(8,128)}, u32[]{:S(2)}, u32[]{:S(2)}) collective-permute-start(f32[16,3072]{1,0:T(8,128)} %fusion), channel_id=1, source_target_pairs={{0,11},{1,12},{2,13},{3,14},{4,15},{5,16},{6,17},{7,18},{8,19},{9,... | collective-permute-start | bytes 589832
  704.5 135.6 %collective-permute-start.11 = (f32[16,3072]{1,0:T(8,128)}, f32[16,3072]{1,0:T(8,128)}, u32[]{:S(2)}, u32[]{:S(2)}) collective-permute-start(f32[16,3072]{1,0:T(8,128)} %fusion), channel_id=1, source_target_pairs={{0,12},{1,13},{2,14},{3,15},{4,16},{5,17},{6,18},{7,19},{8,20},{9,... | collective-permute-start | bytes 589832
  744.4 3.9 copy-start.6
  744.4 99.6 %collective-permute-start.12 = (f32[16,3072]{1,0:T(8,128)}, f32[16,3072]{1,0:T(8,128)}, u32[]{:S(2)}, u32[]{:S(2)}) collective-permute-start(f32[16,3072]{1,0:T(8,128)} %fusion), channel_id=1, source_target_pairs={{0,13},{1,14},{2,15},{3,16},{4,17},{5,18},{6,19},{7,20},{8,21},{9,... | collective-permute-start | bytes 589832
  746.4 2.0 copy-start.4
  746.4 102.5 %collective-permute-start.13 = (f32[16,3072]{1,0:T(8,128)}, f32[16,3072]{1,0:T(8,128)}, u32[]{:S(2)}, u32[]{:S(2)}) collective-permute-start(f32[16,3072]{1,0:T(8,128)} %fusion), channel_id=1, source_target_pairs={{0,14},{1,15},{2,16},{3,17},{4,18},{5,19},{6,20},{7,21},{8,22},{9,... | collective-permute-start | bytes 589832
  821.2 55.2 %all-to-all-start.1 = ((bf16[8,2,16384]{2,1,0:T(2,128)(2,1)}), bf16[8,2,16384]{2,1,0:T(2,128)(2,1)S(1)}, u32[]{:S(2)}, u32[]{:S(2)}) async-start(bf16[8,2,16384]{2,1,0:T(2,128)(2,1)} %reshape.83), calls=%async_computation.1 | async-start | bytes 1048576 | tf_op jit(solution)/shard_map/all_to_all | solution.py:122
  824.7 26.4 %collective-permute-start.14 = (f32[16,3072]{1,0:T(8,128)}, f32[16,3072]{1,0:T(8,128)}, u32[]{:S(2)}, u32[]{:S(2)}) collective-permute-start(f32[16,3072]{1,0:T(8,128)} %fusion), channel_id=1, source_target_pairs={{0,15},{1,16},{2,17},{3,18},{4,19},{5,20},{6,21},{7,22},{8,23},{9,... | collective-permute-start | bytes 589832
  838.1 15.0 %collective-permute-start.15 = (f32[16,3072]{1,0:T(8,128)}, f32[16,3072]{1,0:T(8,128)}, u32[]{:S(2)}, u32[]{:S(2)}) collective-permute-start(f32[16,3072]{1,0:T(8,128)} %fusion), channel_id=1, source_target_pairs={{0,16},{1,17},{2,18},{3,19},{4,20},{5,21},{6,22},{7,23},{8,24},{9,... | collective-permute-start | bytes 589832
  840.1 23.0 %collective-permute-start.16 = (f32[16,3072]{1,0:T(8,128)}, f32[16,3072]{1,0:T(8,128)}, u32[]{:S(2)}, u32[]{:S(2)}) collective-permute-start(f32[16,3072]{1,0:T(8,128)} %fusion), channel_id=1, source_target_pairs={{0,17},{1,18},{2,19},{3,20},{4,21},{5,22},{6,23},{7,24},{8,25},{9,... | collective-permute-start | bytes 589832
  844.0 24.8 %collective-permute-start.17 = (f32[16,3072]{1,0:T(8,128)}, f32[16,3072]{1,0:T(8,128)}, u32[]{:S(2)}, u32[]{:S(2)}) collective-permute-start(f32[16,3072]{1,0:T(8,128)} %fusion), channel_id=1, source_target_pairs={{0,18},{1,19},{2,20},{3,21},{4,22},{5,23},{6,24},{7,25},{8,26},{9,... | collective-permute-start | bytes 589832
  848.9 25.6 %collective-permute-start.18 = (f32[16,3072]{1,0:T(8,128)}, f32[16,3072]{1,0:T(8,128)}, u32[]{:S(2)}, u32[]{:S(2)}) collective-permute-start(f32[16,3072]{1,0:T(8,128)} %fusion), channel_id=1, source_target_pairs={{0,19},{1,20},{2,21},{3,22},{4,23},{5,24},{6,25},{7,26},{8,27},{9,... | collective-permute-start | bytes 589832
  851.2 29.6 %collective-permute-start.19 = (f32[16,3072]{1,0:T(8,128)}, f32[16,3072]{1,0:T(8,128)}, u32[]{:S(2)}, u32[]{:S(2)}) collective-permute-start(f32[16,3072]{1,0:T(8,128)} %fusion), channel_id=1, source_target_pairs={{0,20},{1,21},{2,22},{3,23},{4,24},{5,25},{6,26},{7,27},{8,28},{9,... | collective-permute-start | bytes 589832
  853.1 29.7 %collective-permute-start.2 = (f32[16,3072]{1,0:T(8,128)}, f32[16,3072]{1,0:T(8,128)}, u32[]{:S(2)}, u32[]{:S(2)}) collective-permute-start(f32[16,3072]{1,0:T(8,128)} %fusion), channel_id=1, source_target_pairs={{0,3},{1,4},{2,5},{3,6},{4,7},{5,8},{6,9},{7,10},{8,11},{9,12},{10... | collective-permute-start | bytes 589832
  863.1 21.7 %collective-permute-start.20 = (f32[16,3072]{1,0:T(8,128)}, f32[16,3072]{1,0:T(8,128)}, u32[]{:S(2)}, u32[]{:S(2)}) collective-permute-start(f32[16,3072]{1,0:T(8,128)} %fusion), channel_id=1, source_target_pairs={{0,21},{1,22},{2,23},{3,24},{4,25},{5,26},{6,27},{7,28},{8,29},{9,... | collective-permute-start | bytes 589832
  868.9 21.4 %collective-permute-start.21 = (f32[16,3072]{1,0:T(8,128)}, f32[16,3072]{1,0:T(8,128)}, u32[]{:S(2)}, u32[]{:S(2)}) collective-permute-start(f32[16,3072]{1,0:T(8,128)} %fusion), channel_id=1, source_target_pairs={{0,22},{1,23},{2,24},{3,25},{4,26},{5,27},{6,28},{7,29},{8,30},{9,... | collective-permute-start | bytes 589832
  874.5 17.7 %collective-permute-start.22 = (f32[16,3072]{1,0:T(8,128)}, f32[16,3072]{1,0:T(8,128)}, u32[]{:S(2)}, u32[]{:S(2)}) collective-permute-start(f32[16,3072]{1,0:T(8,128)} %fusion), channel_id=1, source_target_pairs={{0,23},{1,24},{2,25},{3,26},{4,27},{5,28},{6,29},{7,30},{8,31},{9,... | collective-permute-start | bytes 589832
  880.8 65.0 %copy-start.5 = (f32[16,3072]{1,0:T(8,128)S(1)}, f32[16,3072]{1,0:T(8,128)}, u32[]{:S(2)}) copy-start(f32[16,3072]{1,0:T(8,128)} %copy-done.4) | copy-start | bytes 589828
  880.8 65.0 %copy-start.7 = (f32[12,3072]{1,0:T(8,128)S(1)}, f32[12,3072]{1,0:T(8,128)}, u32[]{:S(2)}) copy-start(f32[12,3072]{1,0:T(8,128)} %copy-done.6) | copy-start | bytes 442372
  880.8 19.2 %collective-permute-start.23 = (f32[16,3072]{1,0:T(8,128)}, f32[16,3072]{1,0:T(8,128)S(1)}, u32[]{:S(2)}, u32[]{:S(2)}) collective-permute-start(f32[16,3072]{1,0:T(8,128)} %fusion), channel_id=1, source_target_pairs={{0,24},{1,25},{2,26},{3,27},{4,28},{5,29},{6,30},{7,31},{8,32},{9,... | collective-permute-start | bytes 589832
  882.8 19.1 %collective-permute-start.24 = (f32[16,3072]{1,0:T(8,128)}, f32[16,3072]{1,0:T(8,128)S(1)}, u32[]{:S(2)}, u32[]{:S(2)}) collective-permute-start(f32[16,3072]{1,0:T(8,128)} %fusion), channel_id=1, source_target_pairs={{0,25},{1,26},{2,27},{3,28},{4,29},{5,30},{6,31},{7,32},{8,33},{9,... | collective-permute-start | bytes 589832
  884.8 19.1 %collective-permute-start.25 = (f32[16,3072]{1,0:T(8,128)}, f32[16,3072]{1,0:T(8,128)S(1)}, u32[]{:S(2)}, u32[]{:S(2)}) collective-permute-start(f32[16,3072]{1,0:T(8,128)} %fusion), channel_id=1, source_target_pairs={{0,26},{1,27},{2,28},{3,29},{4,30},{5,31},{6,32},{7,33},{8,34},{9,... | collective-permute-start | bytes 589832
  890.3 16.6 %collective-permute-start.26 = (f32[16,3072]{1,0:T(8,128)}, f32[16,3072]{1,0:T(8,128)S(1)}, u32[]{:S(2)}, u32[]{:S(2)}) collective-permute-start(f32[16,3072]{1,0:T(8,128)} %fusion), channel_id=1, source_target_pairs={{0,27},{1,28},{2,29},{3,30},{4,31},{5,32},{6,33},{7,34},{8,35},{9,... | collective-permute-start | bytes 589832
  892.2 16.6 %collective-permute-start.27 = (f32[16,3072]{1,0:T(8,128)}, f32[16,3072]{1,0:T(8,128)S(1)}, u32[]{:S(2)}, u32[]{:S(2)}) collective-permute-start(f32[16,3072]{1,0:T(8,128)} %fusion), channel_id=1, source_target_pairs={{0,28},{1,29},{2,30},{3,31},{4,32},{5,33},{6,34},{7,35},{8,36},{9,... | collective-permute-start | bytes 589832
  900.0 13.4 %collective-permute-start.28 = (f32[16,3072]{1,0:T(8,128)}, f32[16,3072]{1,0:T(8,128)S(1)}, u32[]{:S(2)}, u32[]{:S(2)}) collective-permute-start(f32[16,3072]{1,0:T(8,128)} %fusion), channel_id=1, source_target_pairs={{0,29},{1,30},{2,31},{3,32},{4,33},{5,34},{6,35},{7,36},{8,37},{9,... | collective-permute-start | bytes 589832
  901.9 17.6 %collective-permute-start.29 = (f32[16,3072]{1,0:T(8,128)}, f32[16,3072]{1,0:T(8,128)S(1)}, u32[]{:S(2)}, u32[]{:S(2)}) collective-permute-start(f32[16,3072]{1,0:T(8,128)} %fusion), channel_id=1, source_target_pairs={{0,30},{1,31},{2,32},{3,33},{4,34},{5,35},{6,36},{7,37},{8,38},{9,... | collective-permute-start | bytes 589832
  903.8 20.6 %collective-permute-start.3 = (f32[16,3072]{1,0:T(8,128)}, f32[16,3072]{1,0:T(8,128)S(1)}, u32[]{:S(2)}, u32[]{:S(2)}) collective-permute-start(f32[16,3072]{1,0:T(8,128)} %fusion), channel_id=1, source_target_pairs={{0,4},{1,5},{2,6},{3,7},{4,8},{5,9},{6,10},{7,11},{8,12},{9,13},{1... | collective-permute-start | bytes 589832
  906.9 30.6 %copy-start.8 = (f32[16,3072]{1,0:T(8,128)}, f32[16,3072]{1,0:T(8,128)S(1)}, u32[]{:S(2)}) copy-start(f32[16,3072]{1,0:T(8,128)S(1)} %collective-permute-done.26) | copy-start | bytes 589828
  906.9 21.4 %collective-permute-start.30 = (f32[16,3072]{1,0:T(8,128)}, f32[16,3072]{1,0:T(8,128)S(1)}, u32[]{:S(2)}, u32[]{:S(2)}) collective-permute-start(f32[16,3072]{1,0:T(8,128)} %fusion), channel_id=1, source_target_pairs={{0,31},{1,32},{2,33},{3,34},{4,35},{5,36},{6,37},{7,38},{8,39},{9,... | collective-permute-start | bytes 589832
  908.9 28.6 %copy-start.9 = (f32[16,3072]{1,0:T(8,128)}, f32[16,3072]{1,0:T(8,128)S(1)}, u32[]{:S(2)}) copy-start(f32[16,3072]{1,0:T(8,128)S(1)} %collective-permute-done.27) | copy-start | bytes 589828
  908.9 21.4 %collective-permute-start.4 = (f32[16,3072]{1,0:T(8,128)}, f32[16,3072]{1,0:T(8,128)S(1)}, u32[]{:S(2)}, u32[]{:S(2)}) collective-permute-start(f32[16,3072]{1,0:T(8,128)} %fusion), channel_id=1, source_target_pairs={{0,5},{1,6},{2,7},{3,8},{4,9},{5,10},{6,11},{7,12},{8,13},{9,14},{... | collective-permute-start | bytes 589832
  913.3 24.1 %collective-permute-start.5 = (f32[16,3072]{1,0:T(8,128)}, f32[16,3072]{1,0:T(8,128)S(1)}, u32[]{:S(2)}, u32[]{:S(2)}) collective-permute-start(f32[16,3072]{1,0:T(8,128)} %fusion), channel_id=1, source_target_pairs={{0,6},{1,7},{2,8},{3,9},{4,10},{5,11},{6,12},{7,13},{8,14},{9,15},... | collective-permute-start | bytes 589832
  919.5 18.0 %collective-permute-start.6 = (f32[16,3072]{1,0:T(8,128)}, f32[16,3072]{1,0:T(8,128)S(1)}, u32[]{:S(2)}, u32[]{:S(2)}) collective-permute-start(f32[16,3072]{1,0:T(8,128)} %fusion), channel_id=1, source_target_pairs={{0,7},{1,8},{2,9},{3,10},{4,11},{5,12},{6,13},{7,14},{8,15},{9,16}... | collective-permute-start | bytes 589832
  924.4 13.1 %collective-permute-start.7 = (f32[16,3072]{1,0:T(8,128)}, f32[16,3072]{1,0:T(8,128)S(1)}, u32[]{:S(2)}, u32[]{:S(2)}) collective-permute-start(f32[16,3072]{1,0:T(8,128)} %fusion), channel_id=1, source_target_pairs={{0,8},{1,9},{2,10},{3,11},{4,12},{5,13},{6,14},{7,15},{8,16},{9,17... | collective-permute-start | bytes 589832
  928.3 15.5 %collective-permute-start.8 = (f32[16,3072]{1,0:T(8,128)}, f32[16,3072]{1,0:T(8,128)}, u32[]{:S(2)}, u32[]{:S(2)}) collective-permute-start(f32[16,3072]{1,0:T(8,128)} %fusion), channel_id=1, source_target_pairs={{0,9},{1,10},{2,11},{3,12},{4,13},{5,14},{6,15},{7,16},{8,17},{9,1... | collective-permute-start | bytes 589832
  930.3 15.5 %collective-permute-start.9 = (f32[16,3072]{1,0:T(8,128)}, f32[16,3072]{1,0:T(8,128)}, u32[]{:S(2)}, u32[]{:S(2)}) collective-permute-start(f32[16,3072]{1,0:T(8,128)} %fusion), channel_id=1, source_target_pairs={{0,10},{1,11},{2,12},{3,13},{4,14},{5,15},{6,16},{7,17},{8,18},{9,... | collective-permute-start | bytes 589832
Sparse Core Ops, SparseCore 0:
  9.7 70.7 all-gather.1
where the time goes:
time: 1040 us
  blocking collectives  356 us (34%)
  matrix products  254 us (24%)
  starting transfers between devices  134 us (13%)
  waiting for transfers between devices  127 us (12%)
  local copies, waits for them, and re-layouts  125 us (12%)
  other arithmetic  20.9 us (2%)
  between operations  15.5 us (1%)
    unnamed x1, blocking collectives  325 us
    unnamed x32, starting transfers between devices  120 us
    unnamed x33, local copies, waits for them, and re-layouts  94 us
    dot_general x4, matrix products, backward_one_block(): jnp.einsum('hqk,qhd->khd', score_gradient, query_block, preferred_element...  63.1 us
    all_gather x1, waiting for transfers between devices, body(): weight_full = lax.all_gather(projection, 'fsdp', axis=0, tiled=True)  61.9 us
    dot_general x4, matrix products, backward_one_block(): jnp.einsum('hqk,khd->qhd', score_gradient, key_rows, preferred_element_ty...  57.5 us
    sub x8, matrix products, block_probabilities(): exponentials = jnp.exp(scores - row_peak)  53.7 us
    unnamed x33, waiting for transfers between devices  44.9 us
  transfers between devices with their start and end apart: 36, of which 7 were waited for; matrix products, arithmetic and copies ran while one was open for 9% of the time, Pallas kernels for 0%

commit v1 on v0

--- a/solution.py
+++ b/solution.py
@@ -105,7 +105,9 @@
     standard = centered * inv_std
     normed = standard.astype(jnp.bfloat16)
     valid = jnp.arange(total_rows, dtype=jnp.int32) < length
-    weight_full = lax.all_gather(projection, "fsdp", axis=0, tiled=True)
+    weight_full = jnp.concatenate(
+        lax.all_to_all(jnp.stack([projection] * lax.axis_size("fsdp")), "fsdp", 0, 0), axis=0
+    )
     packed = jnp.dot(normed, weight_full, preferred_element_type=jnp.float32).astype(jnp.bfloat16)
     packed = packed.reshape(local_rows, 3, seq_count, group_width)
     upstream_four = upstream.reshape(local_rows, 1, seq_count, group_width)

time: 1040 us -> 1080 us (1.038)
  waiting for transfers between devices: 127 us -> 170 us
  between operations: 15.5 us -> 2.07 us
    all_to_all x0 -> x1, waiting for transfers between devices: none -> 104 us  [body(): lax.all_to_all(jnp.stack([projection] * lax.axis_size('fsdp')), 'fsdp', 0...]
    all_gather x1 -> x0, waiting for transfers between devices: 61.9 us -> none  [body(): weight_full = lax.all_gather(projection, 'fsdp', axis=0, tiled=True)]
    unnamed x33 -> x37, local copies, waits for them, and re-layouts: 94 us -> 92.8 us
    unnamed x33 -> x32, waiting for transfers between devices: 44.9 us -> 44.1 us
  transfers between devices with their start and end apart: 36 -> 36, of which waited for: 7 -> 8; matrix products, arithmetic and copies ran while one was open for 9% -> 9% of each run, Pallas kernels for 0% -> 0%
where the time goes in v1:
time: 1080 us
  blocking collectives  355 us (33%)
  matrix products  254 us (24%)
  waiting for transfers between devices  170 us (16%)
  starting transfers between devices  139 us (13%)
  local copies, waits for them, and re-layouts  131 us (12%)
  other arithmetic  18.6 us (2%)
    unnamed x1, blocking collectives  326 us
    unnamed x32, starting transfers between devices  120 us
    all_to_all x1, waiting for transfers between devices, body(): lax.all_to_all(jnp.stack([projection] * lax.axis_size('fsdp')), 'fsdp', 0...  104 us
    unnamed x37, local copies, waits for them, and re-layouts  92.8 us
    dot_general x4, matrix products, backward_one_block(): jnp.einsum('hqk,qhd->khd', score_gradient, query_block, preferred_element...  62.9 us
    dot_general x4, matrix products, backward_one_block(): jnp.einsum('hqk,khd->qhd', score_gradient, key_rows, preferred_element_ty...  57.4 us
    sub x8, matrix products, block_probabilities(): exponentials = jnp.exp(scores - row_peak)  53.7 us
    unnamed x32, waiting for transfers between devices  44.1 us
  transfers between devices with their start and end apart: 36, of which 8 were waited for; matrix products, arithmetic and copies ran while one was open for 9% of the time, Pallas kernels for 0%

profile of v1, /device:TPU:2, one launch (start us, length us, event | category | flops | bytes accessed | tf_op | source)
XLA Modules:
  0.0 1075.5 jit_solution(946491165467172992)
XLA Ops:
  0.6 6.5 stack.18
  7.2 5.9 all-to-all-start
  14.7 104.3 %all-to-all-done = bf16[4,384,3072]{2,1,0:T(8,128)(2,1)} async-done(((bf16[4,384,3072]{2,1,0:T(8,128)(2,1)}), bf16[4,384,3072]{2,1,0:T(8,128)(2,1)}, u32[]{:S(2)}, u32[]{:S(2)}) %all-to-all-start) | async-done | bytes 9437216 | tf_op jit(solution)/shard_map/all_to_all | solution.py:109
  119.0 5.8 all-to-all-start.3
  124.8 6.4 fusion.104
  134.7 4.1 all-to-all-start.1
  140.0 19.6 %all-to-all-done.1 = bf16[256,3,8,128]{3,0,1,2:T(8,128)(2,1)S(1)} async-done(((bf16[256,3,8,128]{3,0,1,2:T(8,128)(2,1)}), bf16[256,3,8,128]{3,0,1,2:T(8,128)(2,1)S(1)}, u32[]{:S(2)}, u32[]{:S(2)}) %all-to-all-start.1) | async-done | bytes 1572896 | tf_op jit(solution)/shard_map/all_to_all | solution.py:115
  165.0 196.6 %while.26 = (s32[]{:T(128)}, f32[2048,2,64]{0,2,1:T(8,128)}, f32[2048,2,64]{0,2,1:T(8,128)}, bf16[4,512,2,64]{1,3,2,0:T(8,128)(2,1)S(1)}, s32[4]{0:T(128)S(1)}, ...) while((s32[]{:T(128)}, f32[2048,2,64]{0,2,1:T(8,128)}, ...), condition=%wide.region_10.11_spmd.clone, body=%wide.region_6.10_spmd.clone.sunk | while | flops 1385373696 | bytes 107115288 | solution.py:80
  166.4 4.6 fusion.162
  170.9 6.6 fusion.163
  177.5 14.4 %fusion.166 = bf16[4,512,2,64]{1,3,2,0:T(8,128)(2,1)S(1)} fusion(bf16[4,512,2,64]{1,3,2,0:T(8,128)(2,1)S(1)} %get-tuple-element.351, s32[]{:T(128)} %get-tuple-element.348, bf16[2048,2,64]{0,2,1:T(8,128)(2,1)S(1)} %get-tuple-element.369, f32[2,512,2048]{2,1,0:T(8,128)} %fusion.162, f32[2,512,2048]{2,1,0:T(8,128)} %get-tuple-element.299, ...), kind=kOutput, calls=%fused_computation.43.clone.1 | convolution fusion | flops 283184128 | bytes 34218496 | tf_op jit(solution)/shard_map/while/body/eval_jaxpr/hqk,khd->qhd/dot_general | solution.py:71
  191.9 5.4 fusion.165
  197.3 15.7 %fusion.164 = f32[2048,2,64]{0,2,1:T(8,128)S(1)} fusion(f32[2,512,2048]{2,1,0:T(8,128)} %fusion.162, f32[2048,2,64]{0,2,1:T(8,128)S(1)} %copy-done.2, pred[]{:T(512)S(6)} %compare.3, bf16[2048,2,64]{0,2,1:T(8,128)(2,1)} %get-tuple-element.367, s32[]{:T(128)S(6)} %select_n.71, f32[2,512,2048]{2,1,0:T(8,128)} %get-tuple-element.299, ...), kind=kOutput, calls=%fused_computation.40.clone.1 | convolution fusion | flops 283642880 | bytes 35790852 | tf_op jit(solution)/shard_map/while/body/eval_jaxpr/hqk,qhd->khd/dot_general | solution.py:74
  215.3 4.6 fusion.162
  219.9 6.6 fusion.163
  226.5 14.3 %fusion.166 = bf16[4,512,2,64]{1,3,2,0:T(8,128)(2,1)S(1)} fusion(bf16[4,512,2,64]{1,3,2,0:T(8,128)(2,1)S(1)} %get-tuple-element.351, s32[]{:T(128)} %get-tuple-element.348, bf16[2048,2,64]{0,2,1:T(8,128)(2,1)S(1)} %get-tuple-element.369, f32[2,512,2048]{2,1,0:T(8,128)} %fusion.162, f32[2,512,2048]{2,1,0:T(8,128)} %get-tuple-element.299, ...), kind=kOutput, calls=%fused_computation.43.clone.1 | convolution fusion | flops 283184128 | bytes 34218496 | tf_op jit(solution)/shard_map/while/body/eval_jaxpr/hqk,khd->qhd/dot_general | solution.py:71
  240.8 5.6 fusion.165
  246.5 15.7 %fusion.164 = f32[2048,2,64]{0,2,1:T(8,128)S(1)} fusion(f32[2,512,2048]{2,1,0:T(8,128)} %fusion.162, f32[2048,2,64]{0,2,1:T(8,128)S(1)} %copy-done.2, pred[]{:T(512)S(6)} %compare.3, bf16[2048,2,64]{0,2,1:T(8,128)(2,1)} %get-tuple-element.367, s32[]{:T(128)S(6)} %select_n.71, f32[2,512,2048]{2,1,0:T(8,128)} %get-tuple-element.299, ...), kind=kOutput, calls=%fused_computation.40.clone.1 | convolution fusion | flops 283642880 | bytes 35790852 | tf_op jit(solution)/shard_map/while/body/eval_jaxpr/hqk,qhd->khd/dot_general | solution.py:74
  264.5 4.6 fusion.162
  269.1 6.6 fusion.163
  275.7 14.4 %fusion.166 = bf16[4,512,2,64]{1,3,2,0:T(8,128)(2,1)S(1)} fusion(bf16[4,512,2,64]{1,3,2,0:T(8,128)(2,1)S(1)} %get-tuple-element.351, s32[]{:T(128)} %get-tuple-element.348, bf16[2048,2,64]{0,2,1:T(8,128)(2,1)S(1)} %get-tuple-element.369, f32[2,512,2048]{2,1,0:T(8,128)} %fusion.162, f32[2,512,2048]{2,1,0:T(8,128)} %get-tuple-element.299, ...), kind=kOutput, calls=%fused_computation.43.clone.1 | convolution fusion | flops 283184128 | bytes 34218496 | tf_op jit(solution)/shard_map/while/body/eval_jaxpr/hqk,khd->qhd/dot_general | solution.py:71
  290.1 5.6 fusion.165
  295.7 15.7 %fusion.164 = f32[2048,2,64]{0,2,1:T(8,128)S(1)} fusion(f32[2,512,2048]{2,1,0:T(8,128)} %fusion.162, f32[2048,2,64]{0,2,1:T(8,128)S(1)} %copy-done.2, pred[]{:T(512)S(6)} %compare.3, bf16[2048,2,64]{0,2,1:T(8,128)(2,1)} %get-tuple-element.367, s32[]{:T(128)S(6)} %select_n.71, f32[2,512,2048]{2,1,0:T(8,128)} %get-tuple-element.299, ...), kind=kOutput, calls=%fused_computation.40.clone.1 | convolution fusion | flops 283642880 | bytes 35790852 | tf_op jit(solution)/shard_map/while/body/eval_jaxpr/hqk,qhd->khd/dot_general | solution.py:74
  313.8 4.6 fusion.162
  318.3 6.6 fusion.163
  324.9 14.4 %fusion.166 = bf16[4,512,2,64]{1,3,2,0:T(8,128)(2,1)S(1)} fusion(bf16[4,512,2,64]{1,3,2,0:T(8,128)(2,1)S(1)} %get-tuple-element.351, s32[]{:T(128)} %get-tuple-element.348, bf16[2048,2,64]{0,2,1:T(8,128)(2,1)S(1)} %get-tuple-element.369, f32[2,512,2048]{2,1,0:T(8,128)} %fusion.162, f32[2,512,2048]{2,1,0:T(8,128)} %get-tuple-element.299, ...), kind=kOutput, calls=%fused_computation.43.clone.1 | convolution fusion | flops 283184128 | bytes 34218496 | tf_op jit(solution)/shard_map/while/body/eval_jaxpr/hqk,khd->qhd/dot_general | solution.py:71
  339.3 5.6 fusion.165
  344.9 15.7 %fusion.164 = f32[2048,2,64]{0,2,1:T(8,128)S(1)} fusion(f32[2,512,2048]{2,1,0:T(8,128)} %fusion.162, f32[2048,2,64]{0,2,1:T(8,128)S(1)} %copy-done.2, pred[]{:T(512)S(6)} %compare.3, bf16[2048,2,64]{0,2,1:T(8,128)(2,1)} %get-tuple-element.367, s32[]{:T(128)S(6)} %select_n.71, f32[2,512,2048]{2,1,0:T(8,128)} %get-tuple-element.299, ...), kind=kOutput, calls=%fused_computation.40.clone.1 | convolution fusion | flops 283642880 | bytes 35790852 | tf_op jit(solution)/shard_map/while/body/eval_jaxpr/hqk,qhd->khd/dot_general | solution.py:74
  366.4 3.0 copy.54
  369.4 29.5 %all_to_all.65 = bf16[2048,3,1,128]{3,1,2,0:T(4,128)(2,1)S(1)} all-to-all(bf16[2048,3,1,128]{3,1,2,0:T(4,128)(2,1)S(1)} %copy.54), channel_id=1, replica_groups=mesh['dp'=4,'fsdp'=4,'seq'=8] {'seq'}, dimensions={0} | all-to-all | bytes 3145728 | tf_op jit(solution)/shard_map/all_to_all | solution.py:134
  402.0 8.0 fusion.106
  410.1 325.8 %fusion = f32[16,3072]{1,0:T(8,128)} fusion(f32[1536,3072]{1,0:T(8,128)} %fusion.106), kind=kCustom, calls=%all-reduce-scatter | all-reduce-scatter fusion | flops 6291457 | bytes 19070976
  735.9 3.2 collective-permute-start
  740.0 3.6 collective-permute-start.31
  743.6 3.1 collective-permute-start.1
  748.6 7.0 collective-permute-start.11
  755.7 33.1 %collective-permute-done.31 = f32[12,3072]{1,0:T(8,128)S(1)} collective-permute-done((f32[12,3072]{1,0:T(8,128)S(1)}, f32[12,3072]{1,0:T(8,128)S(1)}, u32[]{:S(2)}, u32[]{:S(2)}) %collective-permute-start.31) | collective-permute-done | bytes 147488
  792.9 52.5 %while.25 = (s32[]{:T(128)}, bf16[4,512,2,64]{1,3,2,0:T(8,128)(2,1)S(1)}, s32[4]{0:T(128)S(1)}, pred[2048]{0:T(1024)(128)(4,1)S(1)}, bf16[2048,2,64]{0,2,1:T(8,1...) while((s32[]{:T(128)}, ...), condition=%wide.region_5.6_spmd, body=%wide.region_2.5_spmd.sunk | while | flops 549586944 | bytes 18099892 | solution.py:42
  794.3 6.8 fusion.152
  801.2 4.8 fusion.153
  807.4 6.8 fusion.152
  814.3 4.8 fusion.153
  820.5 6.8 fusion.152
  827.4 4.8 fusion.153
  833.6 6.8 fusion.152
  840.5 4.8 fusion.153
  847.4 5.0 reshape.103
  852.9 12.6 %reduce.1 = bf16[2048,128]{1,0:T(8,128)(2,1)S(1)} reduce(bf16[2048,1,128]{2,1,0:T(2,128)(2,1)} %reshape.103, bf16[]{:T(256)} %broadcast.131), dimensions={1}, to_apply=%reshape.103.reduce_sub_computation | reduce | bytes 1048578 | tf_op jit(solution)/shard_map/reshape;reshape | solution.py:125
  866.4 3.5 all-to-all-start.2
  869.9 12.5 %collective-permute-start.14 = (f32[16,3072]{1,0:T(8,128)}, f32[16,3072]{1,0:T(8,128)}, u32[]{:S(2)}, u32[]{:S(2)}) collective-permute-start(f32[16,3072]{1,0:T(8,128)} %fusion), channel_id=1, source_target_pairs={{0,15},{1,16},{2,17},{3,18},{4,19},{5,20},{6,21},{7,22},{8,23},{9,... | collective-permute-start | bytes 589832
  884.3 3.9 collective-permute-start.16
  888.3 4.9 collective-permute-start.17
  897.3 10.0 collective-permute-start.2
  907.3 5.8 collective-permute-start.20
  913.1 5.6 collective-permute-start.21
  929.0 5.5 collective-permute-start.25
  938.7 5.5 fusion.109
  948.1 2.8 collective-permute-start.3
  957.6 6.1 collective-permute-start.5
  963.7 4.9 collective-permute-start.6
  968.6 3.9 collective-permute-start.7
  974.5 5.6 collective-permute-start.9
  981.7 6.3 collective-permute-done.8
  990.0 83.8 %concatenate.1 = f32[524,3072]{1,0:T(8,128)} concatenate(f32[12,3072]{1,0:T(8,128)S(1)} %copy-done.9, f32[16,3072]{1,0:T(8,128)S(1)} %collective-permute-done.30, f32[16,3072]{1,0:T(8,128)S(1)} %collective-permute-done.29, f32[16,3072]{1,0:T(8,128)S(1)} %collective-permute-done.28, f32[16,3072]{1,0:T(8,128)} %copy-done.11, f32[16,3072]{1,0:T(8,128)} %copy-done.10, ...), dimensions={0} | concatenate | bytes 12877824
  (145 shorter events, 76.8 us)
Async XLA Ops:
  7.2 5.9 copy-start.4
  7.2 6.9 copy-start
  7.2 111.9 %all-to-all-start = ((bf16[4,384,3072]{2,1,0:T(8,128)(2,1)}), bf16[4,384,3072]{2,1,0:T(8,128)(2,1)}, u32[]{:S(2)}, u32[]{:S(2)}) async-start(bf16[4,384,3072]{2,1,0:T(8,128)(2,1)} %stack.18), calls=%async_computation | async-start | bytes 18874368 | tf_op jit(solution)/shard_map/all_to_all | solution.py:109
  14.3 116.9 %copy-start.12 = (f32[256]{0:T(256)}, f32[256]{0:T(256)S(1)}, u32[]{:S(2)}) copy-start(f32[256]{0:T(256)S(1)} %broadcast_multiply_fusion.2) | copy-start | bytes 3076
  14.7 116.6 %copy-start.14 = (f32[256]{0:T(256)}, f32[256]{0:T(256)S(1)}, u32[]{:S(2)}) copy-start(f32[256]{0:T(256)S(1)} %add_rsqrt_fusion) | copy-start | bytes 3076
  119.0 15.7 %all-to-all-start.3 = ((bf16[256,1,8,128]{0,3,1,2:T(8,128)(2,1)}), bf16[256,1,8,128]{0,3,1,2:T(8,128)(2,1)S(1)}, u32[]{:S(2)}, u32[]{:S(2)}) async-start(bf16[256,1,8,128]{0,3,1,2:T(8,128)(2,1)} %bitcast.14), calls=%async_computation.3 | async-start | bytes 1048576 | tf_op jit(solution)/shard_map/all_to_all | solution.py:116
  134.7 24.9 %all-to-all-start.1 = ((bf16[256,3,8,128]{3,0,1,2:T(8,128)(2,1)}), bf16[256,3,8,128]{3,0,1,2:T(8,128)(2,1)S(1)}, u32[]{:S(2)}, u32[]{:S(2)}) async-start(bf16[256,3,8,128]{3,0,1,2:T(8,128)(2,1)} %copy.46), calls=%async_computation.1 | async-start | bytes 3145728 | tf_op jit(solution)/shard_map/all_to_all | solution.py:115
  191.9 5.4 copy-start.2
  213.0 1.0 copy-start.3
  240.8 5.6 copy-start.2
  262.2 1.0 copy-start.3
  290.1 5.6 copy-start.2
  311.4 1.0 copy-start.3
  339.3 5.6 copy-start.2
  360.7 1.0 copy-start.3
  361.7 3.4 copy-start.5
  365.1 36.9 %copy-start.1 = (bf16[1,256,1536]{2,1,0:T(8,128)(2,1)S(1)}, bf16[1,256,1536]{2,1,0:T(8,128)(2,1)}, u32[]{:S(2)}) copy-start(bf16[1,256,1536]{2,1,0:T(8,128)(2,1)} %param.8) | copy-start | bytes 2359300
  365.1 36.9 %copy-start.13 = (f32[256]{0:T(256)S(1)}, f32[256]{0:T(256)}, u32[]{:S(2)}) copy-start(f32[256]{0:T(256)} %copy-done.12) | copy-start | bytes 3076
  365.1 36.9 %copy-start.15 = (f32[256]{0:T(256)S(1)}, f32[256]{0:T(256)}, u32[]{:S(2)}) copy-start(f32[256]{0:T(256)} %copy-done.14) | copy-start | bytes 3076
  735.9 54.8 %collective-permute-start = (f32[16,3072]{1,0:T(8,128)}, f32[16,3072]{1,0:T(8,128)S(1)}, u32[]{:S(2)}, u32[]{:S(2)}) collective-permute-start(f32[16,3072]{1,0:T(8,128)} %fusion), channel_id=1, source_target_pairs={{0,1},{1,2},{2,3},{3,4},{4,5},{5,6},{6,7},{7,8},{8,9},{9,10},{10,1... | collective-permute-start | bytes 589832
  740.0 48.7 %collective-permute-start.31 = (f32[12,3072]{1,0:T(8,128)S(1)}, f32[12,3072]{1,0:T(8,128)S(1)}, u32[]{:S(2)}, u32[]{:S(2)}) collective-permute-start(f32[12,3072]{1,0:T(8,128)S(1)} %slice.15), channel_id=1, source_target_pairs={{0,32},{1,33},{2,34},{3,35},{4,36},{5,37},{6,38},{7,39},{8,40},{9,... | collective-permute-start | bytes 442376
  743.6 126.3 %collective-permute-start.1 = (f32[16,3072]{1,0:T(8,128)}, f32[16,3072]{1,0:T(8,128)}, u32[]{:S(2)}, u32[]{:S(2)}) collective-permute-start(f32[16,3072]{1,0:T(8,128)} %fusion), channel_id=1, source_target_pairs={{0,2},{1,3},{2,4},{3,5},{4,6},{5,7},{6,8},{7,9},{8,10},{9,11},{10,... | collective-permute-start | bytes 589832
  746.7 135.7 %collective-permute-start.10 = (f32[16,3072]{1,0:T(8,128)}, f32[16,3072]{1,0:T(8,128)}, u32[]{:S(2)}, u32[]{:S(2)}) collective-permute-start(f32[16,3072]{1,0:T(8,128)} %fusion), channel_id=1, source_target_pairs={{0,11},{1,12},{2,13},{3,14},{4,15},{5,16},{6,17},{7,18},{8,19},{9,... | collective-permute-start | bytes 589832
  748.6 135.7 %collective-permute-start.11 = (f32[16,3072]{1,0:T(8,128)}, f32[16,3072]{1,0:T(8,128)}, u32[]{:S(2)}, u32[]{:S(2)}) collective-permute-start(f32[16,3072]{1,0:T(8,128)} %fusion), channel_id=1, source_target_pairs={{0,12},{1,13},{2,14},{3,15},{4,16},{5,17},{6,18},{7,19},{8,20},{9,... | collective-permute-start | bytes 589832
  788.7 4.1 copy-start.8
  788.7 99.5 %collective-permute-start.12 = (f32[16,3072]{1,0:T(8,128)}, f32[16,3072]{1,0:T(8,128)}, u32[]{:S(2)}, u32[]{:S(2)}) collective-permute-start(f32[16,3072]{1,0:T(8,128)} %fusion), channel_id=1, source_target_pairs={{0,13},{1,14},{2,15},{3,16},{4,17},{5,18},{6,19},{7,20},{8,21},{9,... | collective-permute-start | bytes 589832
  790.7 2.2 copy-start.6
  790.7 102.5 %collective-permute-start.13 = (f32[16,3072]{1,0:T(8,128)}, f32[16,3072]{1,0:T(8,128)}, u32[]{:S(2)}, u32[]{:S(2)}) collective-permute-start(f32[16,3072]{1,0:T(8,128)} %fusion), channel_id=1, source_target_pairs={{0,14},{1,15},{2,16},{3,17},{4,18},{5,19},{6,20},{7,21},{8,22},{9,... | collective-permute-start | bytes 589832
  866.4 54.3 %all-to-all-start.2 = ((bf16[8,2,16384]{2,1,0:T(2,128)(2,1)}), bf16[8,2,16384]{2,1,0:T(2,128)(2,1)S(1)}, u32[]{:S(2)}, u32[]{:S(2)}) async-start(bf16[8,2,16384]{2,1,0:T(2,128)(2,1)} %reshape.104), calls=%async_computation.2 | async-start | bytes 1048576 | tf_op jit(solution)/shard_map/all_to_all | solution.py:124
  869.9 25.5 %collective-permute-start.14 = (f32[16,3072]{1,0:T(8,128)}, f32[16,3072]{1,0:T(8,128)}, u32[]{:S(2)}, u32[]{:S(2)}) collective-permute-start(f32[16,3072]{1,0:T(8,128)} %fusion), channel_id=1, source_target_pairs={{0,15},{1,16},{2,17},{3,18},{4,19},{5,20},{6,21},{7,22},{8,23},{9,... | collective-permute-start | bytes 589832
  882.4 15.0 %collective-permute-start.15 = (f32[16,3072]{1,0:T(8,128)}, f32[16,3072]{1,0:T(8,128)}, u32[]{:S(2)}, u32[]{:S(2)}) collective-permute-start(f32[16,3072]{1,0:T(8,128)} %fusion), channel_id=1, source_target_pairs={{0,16},{1,17},{2,18},{3,19},{4,20},{5,21},{6,22},{7,23},{8,24},{9,... | collective-permute-start | bytes 589832
  884.3 23.0 %collective-permute-start.16 = (f32[16,3072]{1,0:T(8,128)}, f32[16,3072]{1,0:T(8,128)}, u32[]{:S(2)}, u32[]{:S(2)}) collective-permute-start(f32[16,3072]{1,0:T(8,128)} %fusion), channel_id=1, source_target_pairs={{0,17},{1,18},{2,19},{3,20},{4,21},{5,22},{6,23},{7,24},{8,25},{9,... | collective-permute-start | bytes 589832
  888.3 24.9 %collective-permute-start.17 = (f32[16,3072]{1,0:T(8,128)}, f32[16,3072]{1,0:T(8,128)}, u32[]{:S(2)}, u32[]{:S(2)}) collective-permute-start(f32[16,3072]{1,0:T(8,128)} %fusion), channel_id=1, source_target_pairs={{0,18},{1,19},{2,20},{3,21},{4,22},{5,23},{6,24},{7,25},{8,26},{9,... | collective-permute-start | bytes 589832
  893.1 25.6 %collective-permute-start.18 = (f32[16,3072]{1,0:T(8,128)}, f32[16,3072]{1,0:T(8,128)}, u32[]{:S(2)}, u32[]{:S(2)}) collective-permute-start(f32[16,3072]{1,0:T(8,128)} %fusion), channel_id=1, source_target_pairs={{0,19},{1,20},{2,21},{3,22},{4,23},{5,24},{6,25},{7,26},{8,27},{9,... | collective-permute-start | bytes 589832
  895.4 29.6 %collective-permute-start.19 = (f32[16,3072]{1,0:T(8,128)}, f32[16,3072]{1,0:T(8,128)}, u32[]{:S(2)}, u32[]{:S(2)}) collective-permute-start(f32[16,3072]{1,0:T(8,128)} %fusion), channel_id=1, source_target_pairs={{0,20},{1,21},{2,22},{3,23},{4,24},{5,25},{6,26},{7,27},{8,28},{9,... | collective-permute-start | bytes 589832
  897.3 29.7 %collective-permute-start.2 = (f32[16,3072]{1,0:T(8,128)}, f32[16,3072]{1,0:T(8,128)}, u32[]{:S(2)}, u32[]{:S(2)}) collective-permute-start(f32[16,3072]{1,0:T(8,128)} %fusion), channel_id=1, source_target_pairs={{0,3},{1,4},{2,5},{3,6},{4,7},{5,8},{6,9},{7,10},{8,11},{9,12},{10... | collective-permute-start | bytes 589832
  907.3 21.7 %collective-permute-start.20 = (f32[16,3072]{1,0:T(8,128)}, f32[16,3072]{1,0:T(8,128)}, u32[]{:S(2)}, u32[]{:S(2)}) collective-permute-start(f32[16,3072]{1,0:T(8,128)} %fusion), channel_id=1, source_target_pairs={{0,21},{1,22},{2,23},{3,24},{4,25},{5,26},{6,27},{7,28},{8,29},{9,... | collective-permute-start | bytes 589832
  913.1 21.4 %collective-permute-start.21 = (f32[16,3072]{1,0:T(8,128)}, f32[16,3072]{1,0:T(8,128)}, u32[]{:S(2)}, u32[]{:S(2)}) collective-permute-start(f32[16,3072]{1,0:T(8,128)} %fusion), channel_id=1, source_target_pairs={{0,22},{1,23},{2,24},{3,25},{4,26},{5,27},{6,28},{7,29},{8,30},{9,... | collective-permute-start | bytes 589832
  918.7 17.7 %collective-permute-start.22 = (f32[16,3072]{1,0:T(8,128)}, f32[16,3072]{1,0:T(8,128)}, u32[]{:S(2)}, u32[]{:S(2)}) collective-permute-start(f32[16,3072]{1,0:T(8,128)} %fusion), channel_id=1, source_target_pairs={{0,23},{1,24},{2,25},{3,26},{4,27},{5,28},{6,29},{7,30},{8,31},{9,... | collective-permute-start | bytes 589832
  925.0 65.0 %copy-start.7 = (f32[16,3072]{1,0:T(8,128)S(1)}, f32[16,3072]{1,0:T(8,128)}, u32[]{:S(2)}) copy-start(f32[16,3072]{1,0:T(8,128)} %copy-done.6) | copy-start | bytes 589828
  925.0 65.0 %copy-start.9 = (f32[12,3072]{1,0:T(8,128)S(1)}, f32[12,3072]{1,0:T(8,128)}, u32[]{:S(2)}) copy-start(f32[12,3072]{1,0:T(8,128)} %copy-done.8) | copy-start | bytes 442372
  925.0 19.2 %collective-permute-start.23 = (f32[16,3072]{1,0:T(8,128)}, f32[16,3072]{1,0:T(8,128)S(1)}, u32[]{:S(2)}, u32[]{:S(2)}) collective-permute-start(f32[16,3072]{1,0:T(8,128)} %fusion), channel_id=1, source_target_pairs={{0,24},{1,25},{2,26},{3,27},{4,28},{5,29},{6,30},{7,31},{8,32},{9,... | collective-permute-start | bytes 589832
  927.1 19.0 %collective-permute-start.24 = (f32[16,3072]{1,0:T(8,128)}, f32[16,3072]{1,0:T(8,128)S(1)}, u32[]{:S(2)}, u32[]{:S(2)}) collective-permute-start(f32[16,3072]{1,0:T(8,128)} %fusion), channel_id=1, source_target_pairs={{0,25},{1,26},{2,27},{3,28},{4,29},{5,30},{6,31},{7,32},{8,33},{9,... | collective-permute-start | bytes 589832
  929.0 19.0 %collective-permute-start.25 = (f32[16,3072]{1,0:T(8,128)}, f32[16,3072]{1,0:T(8,128)S(1)}, u32[]{:S(2)}, u32[]{:S(2)}) collective-permute-start(f32[16,3072]{1,0:T(8,128)} %fusion), channel_id=1, source_target_pairs={{0,26},{1,27},{2,28},{3,29},{4,30},{5,31},{6,32},{7,33},{8,34},{9,... | collective-permute-start | bytes 589832
  934.5 16.6 %collective-permute-start.26 = (f32[16,3072]{1,0:T(8,128)}, f32[16,3072]{1,0:T(8,128)S(1)}, u32[]{:S(2)}, u32[]{:S(2)}) collective-permute-start(f32[16,3072]{1,0:T(8,128)} %fusion), channel_id=1, source_target_pairs={{0,27},{1,28},{2,29},{3,30},{4,31},{5,32},{6,33},{7,34},{8,35},{9,... | collective-permute-start | bytes 589832
  936.5 16.6 %collective-permute-start.27 = (f32[16,3072]{1,0:T(8,128)}, f32[16,3072]{1,0:T(8,128)S(1)}, u32[]{:S(2)}, u32[]{:S(2)}) collective-permute-start(f32[16,3072]{1,0:T(8,128)} %fusion), channel_id=1, source_target_pairs={{0,28},{1,29},{2,30},{3,31},{4,32},{5,33},{6,34},{7,35},{8,36},{9,... | collective-permute-start | bytes 589832
  944.2 13.4 %collective-permute-start.28 = (f32[16,3072]{1,0:T(8,128)}, f32[16,3072]{1,0:T(8,128)S(1)}, u32[]{:S(2)}, u32[]{:S(2)}) collective-permute-start(f32[16,3072]{1,0:T(8,128)} %fusion), channel_id=1, source_target_pairs={{0,29},{1,30},{2,31},{3,32},{4,33},{5,34},{6,35},{7,36},{8,37},{9,... | collective-permute-start | bytes 589832
  946.1 17.6 %collective-permute-start.29 = (f32[16,3072]{1,0:T(8,128)}, f32[16,3072]{1,0:T(8,128)S(1)}, u32[]{:S(2)}, u32[]{:S(2)}) collective-permute-start(f32[16,3072]{1,0:T(8,128)} %fusion), channel_id=1, source_target_pairs={{0,30},{1,31},{2,32},{3,33},{4,34},{5,35},{6,36},{7,37},{8,38},{9,... | collective-permute-start | bytes 589832
  948.1 20.6 %collective-permute-start.3 = (f32[16,3072]{1,0:T(8,128)}, f32[16,3072]{1,0:T(8,128)S(1)}, u32[]{:S(2)}, u32[]{:S(2)}) collective-permute-start(f32[16,3072]{1,0:T(8,128)} %fusion), channel_id=1, source_target_pairs={{0,4},{1,5},{2,6},{3,7},{4,8},{5,9},{6,10},{7,11},{8,12},{9,13},{1... | collective-permute-start | bytes 589832
  951.2 30.5 %copy-start.10 = (f32[16,3072]{1,0:T(8,128)}, f32[16,3072]{1,0:T(8,128)S(1)}, u32[]{:S(2)}) copy-start(f32[16,3072]{1,0:T(8,128)S(1)} %collective-permute-done.26) | copy-start | bytes 589828
  951.2 21.4 %collective-permute-start.30 = (f32[16,3072]{1,0:T(8,128)}, f32[16,3072]{1,0:T(8,128)S(1)}, u32[]{:S(2)}, u32[]{:S(2)}) collective-permute-start(f32[16,3072]{1,0:T(8,128)} %fusion), channel_id=1, source_target_pairs={{0,31},{1,32},{2,33},{3,34},{4,35},{5,36},{6,37},{7,38},{8,39},{9,... | collective-permute-start | bytes 589832
  953.1 28.6 %copy-start.11 = (f32[16,3072]{1,0:T(8,128)}, f32[16,3072]{1,0:T(8,128)S(1)}, u32[]{:S(2)}) copy-start(f32[16,3072]{1,0:T(8,128)S(1)} %collective-permute-done.27) | copy-start | bytes 589828
  953.1 21.4 %collective-permute-start.4 = (f32[16,3072]{1,0:T(8,128)}, f32[16,3072]{1,0:T(8,128)S(1)}, u32[]{:S(2)}, u32[]{:S(2)}) collective-permute-start(f32[16,3072]{1,0:T(8,128)} %fusion), channel_id=1, source_target_pairs={{0,5},{1,6},{2,7},{3,8},{4,9},{5,10},{6,11},{7,12},{8,13},{9,14},{... | collective-permute-start | bytes 589832
  957.6 24.1 %collective-permute-start.5 = (f32[16,3072]{1,0:T(8,128)}, f32[16,3072]{1,0:T(8,128)S(1)}, u32[]{:S(2)}, u32[]{:S(2)}) collective-permute-start(f32[16,3072]{1,0:T(8,128)} %fusion), channel_id=1, source_target_pairs={{0,6},{1,7},{2,8},{3,9},{4,10},{5,11},{6,12},{7,13},{8,14},{9,15},... | collective-permute-start | bytes 589832
  963.7 18.0 %collective-permute-start.6 = (f32[16,3072]{1,0:T(8,128)}, f32[16,3072]{1,0:T(8,128)S(1)}, u32[]{:S(2)}, u32[]{:S(2)}) collective-permute-start(f32[16,3072]{1,0:T(8,128)} %fusion), channel_id=1, source_target_pairs={{0,7},{1,8},{2,9},{3,10},{4,11},{5,12},{6,13},{7,14},{8,15},{9,16}... | collective-permute-start | bytes 589832
  968.6 13.1 %collective-permute-start.7 = (f32[16,3072]{1,0:T(8,128)}, f32[16,3072]{1,0:T(8,128)S(1)}, u32[]{:S(2)}, u32[]{:S(2)}) collective-permute-start(f32[16,3072]{1,0:T(8,128)} %fusion), channel_id=1, source_target_pairs={{0,8},{1,9},{2,10},{3,11},{4,12},{5,13},{6,14},{7,15},{8,16},{9,17... | collective-permute-start | bytes 589832
  972.6 15.5 %collective-permute-start.8 = (f32[16,3072]{1,0:T(8,128)}, f32[16,3072]{1,0:T(8,128)}, u32[]{:S(2)}, u32[]{:S(2)}) collective-permute-start(f32[16,3072]{1,0:T(8,128)} %fusion), channel_id=1, source_target_pairs={{0,9},{1,10},{2,11},{3,12},{4,13},{5,14},{6,15},{7,16},{8,17},{9,1... | collective-permute-start | bytes 589832
  974.5 15.5 %collective-permute-start.9 = (f32[16,3072]{1,0:T(8,128)}, f32[16,3072]{1,0:T(8,128)}, u32[]{:S(2)}, u32[]{:S(2)}) collective-permute-start(f32[16,3072]{1,0:T(8,128)} %fusion), channel_id=1, source_target_pairs={{0,10},{1,11},{2,12},{3,13},{4,14},{5,15},{6,16},{7,17},{8,18},{9,... | collective-permute-start | bytes 589832
